TPU v7x, 32 devices: a whole 2x2x4 slice. The times are simulated.
32 devices in a mesh: section: 4 (over x, core), tensor: 8 (over z, y).
Axes of the slice: x: 2, y: 2, z: 4, core: 2. Of those that a mesh axis runs over, the one named last changes fastest.
Arguments:
- context: bfloat16 [4, 256, 1024], P('section', None, 'tensor'), may hold values from -6 to 6
- out_weight: bfloat16 [4, 1024, 8192], P('section', 'tensor'), may hold values from -0.1875 to 0.1875
- residual: bfloat16 [4, 256, 8192], P('section', None, 'tensor'), may hold values from -36 to 36
- gain: float32 [4, 8192], P('section', 'tensor'), may hold values from 0.1 to 1.9
- q_weight: bfloat16 [4, 8192, 1024], P('section', None, 'tensor'), may hold values from -0.044194174 to 0.044194174
- kv_weight: bfloat16 [4, 8192, 256], P('section', None, 'tensor'), may hold values from -0.044194174 to 0.044194174
Outputs:
- attended: bfloat16 [4, 256, 1024], P('section', None, 'tensor')
All inputs are finite; a program needn't handle non-finite values.
Results may differ from a plain program's by a relative error of at most 0.033.
Values may be sent and summed in bfloat16 or wider, within the bound.
A program may use at most 64 MiB of HBM per device.

v0:
```python
import jax
import jax.numpy as jnp
from jax import lax
from jax.sharding import PartitionSpec as P

GROUP = 8


THETA = 500000.0


def passed_along(block, axis, distance):
    devices = range(lax.axis_size(axis))
    route = [((i - distance) % len(devices), i) for i in devices]
    return lax.ppermute(block, axis, route)


def rotate(inputs, positions):
    half_width = inputs.shape[-1] // 2
    frequency = THETA ** (-(jnp.arange(half_width).astype(jnp.float32) * 2.0 / inputs.shape[-1]))
    angles = positions[:, None] * frequency[None, :]
    cosine = jnp.cos(angles)[:, None, :]
    sine_part = jnp.sin(angles)[:, None, :]
    first_half = inputs[..., :half_width]
    second_half = inputs[..., half_width:]
    return jnp.concatenate(
        [
            first_half * cosine - second_half * sine_part,
            second_half * cosine + first_half * sine_part,
        ],
        axis=-1,
    )


def on_device(context, out_weight, residual, gain, q_weight, kv_weight):
    local_context = context[0]
    local_out = out_weight[0]
    terms = jnp.dot(local_context, local_out, preferred_element_type=jnp.float32)
    summed = lax.psum_scatter(
        terms.astype(jnp.bfloat16), "tensor", scatter_dimension=1, tiled=True
    ).astype(jnp.float32)
    combined = (residual[0].astype(jnp.float32) + summed).astype(jnp.bfloat16)
    section_gain = gain[0]
    query_cols = q_weight[0]
    pair_cols = kv_weight[0]
    head_size = query_cols.shape[1]
    length = combined.shape[0]
    gathered = lax.all_gather(combined, "tensor", axis=1, tiled=True)
    shifted = passed_along(gathered, "section", 1)
    full_gain = lax.all_gather(section_gain, "tensor", axis=0, tiled=True)
    values_f = shifted.astype(jnp.float32)
    normed = (
        values_f
        * lax.rsqrt(jnp.mean(values_f * values_f, axis=-1, keepdims=True) + 1e-05)
        * full_gain[None, :]
    ).astype(jnp.bfloat16)
    query_proj = jnp.dot(normed, query_cols, preferred_element_type=jnp.float32)
    pair_proj = jnp.dot(normed, pair_cols, preferred_element_type=jnp.float32)
    positions = jnp.arange(length).astype(jnp.float32)
    queries = rotate(query_proj[:, None, :], positions)[:, 0].astype(jnp.bfloat16)
    pair_part = pair_proj.astype(jnp.bfloat16)
    all_pairs = lax.all_gather(pair_part, "tensor", axis=1, tiled=True)
    group_count = lax.axis_size("tensor")
    feature_share = head_size // group_count
    kv_total = pair_cols.shape[1] * group_count // (2 * head_size)
    group_index = lax.axis_index("tensor") // GROUP
    split_cols = all_pairs.reshape(length, group_count, kv_total, 2 * feature_share)
    picked = lax.dynamic_index_in_dim(split_cols, group_index, 2, keepdims=False)
    picked = jnp.transpose(
        picked.reshape(length, group_count, 2, feature_share), (0, 2, 1, 3)
    ).reshape(length, 2, head_size)
    key_rows = rotate(picked[:, 0:1].astype(jnp.float32), positions)[:, 0].astype(jnp.bfloat16)
    values = picked[:, 1]
    scores = jnp.einsum(
        "sd,td->st", queries, key_rows, preferred_element_type=jnp.float32
    ) * head_size ** (-0.5)
    order = jnp.arange(length)
    causal = order[:, None] >= order[None, :]
    scores = jnp.where(causal, scores, -1e30)
    softmax_weights = jax.nn.softmax(scores, axis=-1).astype(jnp.bfloat16)
    attended = jnp.dot(softmax_weights, values, preferred_element_type=jnp.float32).astype(
        jnp.bfloat16
    )
    return attended[None]


def solution(mesh):
    placed = (
        P("section", None, "tensor"),
        P("section", "tensor", None),
        P("section", None, "tensor"),
        P("section", "tensor"),
        P("section", None, "tensor"),
        P("section", None, "tensor"),
    )
    return jax.shard_map(
        on_device,
        mesh=mesh,
        in_specs=placed,
        out_specs=P("section", None, "tensor"),
        check_vma=False,
    )
```

profile of v0, /device:TPU:0, one launch (start us, length us, event | category | flops | bytes accessed | tf_op | source)
XLA Modules:
  0.0 270.3 jit_solution(12673550103402193595)
XLA Ops:
  6.5 0.0 copy-start
  6.5 0.0 reduce-scatter.2.cloned.1.call-start
  6.5 1.6 copy-done
  8.1 4.0 %convolution_convert_fusion = bf16[256,8192]{1,0:T(8,128)(2,1)} fusion(bf16[1,128,8192]{2,1,0:T(8,128)(2,1)S(1)} %copy-done, bf16[1,256,128]{2,1,0:T(8,128)(2,1)} %param.6), kind=kOutput, calls=%fused_computation.2 | convolution fusion | flops 538968064 | bytes 6356992 | tf_op jit(solution)/shard_map/dot_general | solution.py:38
  12.1 0.0 reduce-scatter.2.cloned.1.call-update
  12.2 0.0 copy-start.4
  12.2 0.0 all-gather.3.cloned.1.call-start
  12.2 91.3 %reduce-scatter.2.cloned.1.call-done = bf16[256,1024]{1,0:T(8,128)(2,1)} async-done(((bf16[256,8192]{1,0:T(8,128)(2,1)}), bf16[256,1024]{1,0:T(8,128)(2,1)}) %reduce-scatter.2.cloned.1.call-update) | async-done | bytes 524304 | tf_op jit(solution)/shard_map/reduce_scatter | solution.py:39
  103.5 2.1 fusion.19
  105.5 0.0 all-gather.3.cloned.1.call-update
  105.6 73.5 %all-gather.3.cloned.1.call-done = bf16[256,8192]{1,0:T(8,128)(2,1)} async-done(((bf16[256,1024]{1,0:T(8,128)(2,1)}), bf16[256,8192]{1,0:T(8,128)(2,1)}) %all-gather.3.cloned.1.call-update) | async-done | bytes 4194320 | tf_op jit(solution)/shard_map/all_gather | solution.py:48
  179.1 0.0 collective-permute-start
  179.1 30.4 %all-gather = f32[1,8192]{1,0:T(1,128)S(1)} all-gather(f32[1,1024]{1,0:T(1,128)S(1)} %copy-done.2), channel_id=2, replica_groups=mesh['section'=4,'tensor'=8] {'tensor'}, dimensions={1}, use_global_device_ids=true | all-gather | bytes 36864 | tf_op jit(solution)/shard_map/all_gather | solution.py:50
  209.5 17.7 %collective-permute-done = bf16[256,8192]{1,0:T(8,128)(2,1)S(1)} collective-permute-done((bf16[256,8192]{1,0:T(8,128)(2,1)}, bf16[256,8192]{1,0:T(8,128)(2,1)S(1)}, u32[]{:S(2)}, u32[]{:S(2)}) %collective-permute-start) | collective-permute-done | bytes 4194336 | tf_op jit(solution)/shard_map/ppermute | solution.py:15
  227.2 0.9 fusion
  228.1 0.0 copy-done.4
  228.1 0.0 copy-start.3
  228.1 1.4 fusion.16
  229.6 30.6 %all_gather.11 = bf16[256,256]{0,1:T(8,128)(2,1)S(1)} all-gather(bf16[256,32]{0,1:T(8,128)(2,1)S(1)} %fusion.16), channel_id=1, replica_groups=mesh['section'=4,'tensor'=8] {'tensor'}, dimensions={1}, use_global_device_ids=true | all-gather | bytes 147456 | tf_op jit(solution)/shard_map/all_gather | solution.py:62
  260.2 1.7 fusion.10
  261.9 0.3 fusion.46
  262.3 0.3 fusion.50
  262.5 0.1 fusion.21
  262.6 0.9 fusion.15
  (10 shorter events, 0.0 us)
Async XLA Ops:
  6.5 1.6 copy-start
  6.5 96.9 %copy-start.1 = (bf16[1,256,1024]{2,1,0:T(8,128)(2,1)S(1)}, bf16[1,256,1024]{2,1,0:T(8,128)(2,1)}, u32[]{:S(2)}) copy-start(bf16[1,256,1024]{2,1,0:T(8,128)(2,1)} %param.8) | copy-start | bytes 1572868
  6.5 96.9 %reduce-scatter.2.cloned.1.call-start = ((), (), s32[]{:S(2)}) async-start(), calls=%async_computation.1 | async-start | bytes 4718592 | tf_op jit(solution)/shard_map/reduce_scatter | solution.py:39
  12.1 166.9 %copy-start.2 = (f32[1,1024]{1,0:T(1,128)S(1)}, f32[1,1024]{1,0:T(1,128)}, u32[]{:S(2)}) copy-start(f32[1,1024]{1,0:T(1,128)} %param.9) | copy-start | bytes 12292
  12.2 216.0 %copy-start.4 = (bf16[1,8192,32]{1,2,0:T(8,128)(2,1)S(1)}, bf16[1,8192,32]{1,2,0:T(8,128)(2,1)}, u32[]{:S(2)}) copy-start(bf16[1,8192,32]{1,2,0:T(8,128)(2,1)} %param.11) | copy-start | bytes 1572868
  12.2 166.9 %all-gather.3.cloned.1.call-start = ((), (), s32[]{:S(2)}) async-start(), calls=%async_computation.2 | async-start | bytes 4718592 | tf_op jit(solution)/shard_map/all_gather | solution.py:48
  179.1 48.1 %collective-permute-start = (bf16[256,8192]{1,0:T(8,128)(2,1)}, bf16[256,8192]{1,0:T(8,128)(2,1)S(1)}, u32[]{:S(2)}, u32[]{:S(2)}) collective-permute-start(bf16[256,8192]{1,0:T(8,128)(2,1)} %all-gather.3.cloned.1.call-done), channel_id=1, source_target_pairs={{24,0},{0,8},{8,16},{16,24},{25,1},{1,9},{9,17},{17,25},{26,2},{2,... | collective-permute-start | bytes 12582920 | tf_op jit(solution)/shard_map/ppermute | solution.py:15
  228.1 32.0 %copy-start.3 = (bf16[1,8192,128]{2,1,0:T(8,128)(2,1)S(1)}, bf16[1,8192,128]{2,1,0:T(8,128)(2,1)}, u32[]{:S(2)}) copy-start(bf16[1,8192,128]{2,1,0:T(8,128)(2,1)} %param.10) | copy-start | bytes 6291460
Sparse Core Ops, SparseCore 0:
  12.3 91.1 reduce-scatter.1
  105.9 73.1 all-gather.2
where the time goes:
time: 271 us; the launch traced here: 270 us
  waiting for transfers between devices  183 us (68%)
  blocking collectives  61 us (23%)
  between operations  13.5 us (5%)
  matrix products  8.32 us (3%)
  other arithmetic  3.42 us (1%)
    reduce_scatter x1, waiting for transfers between devices, on_device(): lax.psum_scatter(terms.astype(jnp.bfloat16), 'tensor', scatter_dimension=...  91.3 us
    all_gather x1, waiting for transfers between devices, on_device(): gathered = lax.all_gather(combined, 'tensor', axis=1, tiled=True)  73.5 us
    all_gather x1, blocking collectives, on_device(): all_pairs = lax.all_gather(pair_part, 'tensor', axis=1, tiled=True)  30.6 us
    all_gather x1, blocking collectives, on_device(): full_gain = lax.all_gather(section_gain, 'tensor', axis=0, tiled=True)  30.4 us
    ppermute x1, waiting for transfers between devices, passed_along(): return lax.ppermute(block, axis, route)  17.7 us
  transfers between devices with their start and end apart: 3, of which 3 were waited for; matrix products, arithmetic and copies ran while one was open for 0% of the time, Pallas kernels for 0%

commit v1 on v0

v1 whole, which is shorter than its diff:
```python
import functools

import jax
import jax.numpy as jnp
import numpy as np
from jax import lax
from jax.experimental import pallas as pl
from jax.experimental.pallas import tpu as pltpu
from jax.sharding import PartitionSpec as P

GROUP = 8
THETA = 500000.0
EPS = 1e-05
MESH = pl.DeviceIdType.MESH
BF16 = jnp.bfloat16
F32 = jnp.float32
NG = 4


def rope_tables(length, head_size):
    half = head_size // 2
    frequency = np.float32(THETA) ** (-(np.arange(half, dtype=np.float32) * np.float32(2.0) / np.float32(head_size)))
    angles = np.arange(length, dtype=np.float32)[:, None] * frequency.astype(np.float32)[None, :]
    cosine, sine = np.cos(angles).astype(np.float32), np.sin(angles).astype(np.float32)
    return (
        np.concatenate([cosine, cosine], axis=1),
        np.concatenate([-sine, sine], axis=1),
        np.ascontiguousarray(np.concatenate([cosine, cosine], axis=1).T),
        np.ascontiguousarray(np.concatenate([-sine, sine], axis=1).T),
    )


def dot_nt(a, b):
    return lax.dot_general(a, b, (((1,), (1,)), ((), ())), preferred_element_type=F32)


def kernel(
    T, S,
    ctx, res, gain, cos_q, sin_q, cos_k, sin_k, ow_hbm, qw_hbm, kvw_hbm,
    out,
    ow, kvw, w, first, rs, hand, xb, gains, acc, ssq, kvall,
    load_sem, rs_send, rs_recv, sh_send, sh_recv, ag_send, ag_recv, g_send, g_recv, kv_send, kv_recv,
):
    L, HD = ctx.shape
    B = res.shape[1]
    D = ow.shape[1]
    KC = kvw.shape[1]
    R = L // NG
    half = L // 2
    sec = lax.axis_index("section")
    me = lax.axis_index("tensor")

    def ring(pos):
        upper = pos // (T // 2)
        return (1 - upper) * (2 * pos) + upper * (2 * (T - 1 - pos) + 1)

    y = me % 2
    p = (1 - y) * (me // 2) + y * (T - 1 - me // 2)

    def at(offset):
        return ring((p + offset + 2 * T) % T)

    sides = (at(1), at(-1))
    signs = (1, -1)
    side_of = [0 if g < NG // 2 else 1 for g in range(NG)]
    following = (sec + 1) % S
    previous = (sec + S - 1) % S

    loads = [
        pltpu.make_async_copy(ow_hbm, ow, load_sem.at[0]),
        pltpu.make_async_copy(kvw_hbm, kvw, load_sem.at[1]),
        pltpu.make_async_copy(qw_hbm, w.at[:, pl.ds(0, HD)], load_sem.at[2]),
    ]
    for load in loads:
        load.start()

    barrier = pltpu.get_barrier_semaphore()

    def greet(j, c):
        pl.semaphore_signal(barrier, inc=1, device_id=(sec, (me + j) % T), device_id_type=MESH)
        return c

    lax.fori_loop(1, T, greet, 0)
    pl.semaphore_signal(barrier, inc=1, device_id=(following, me), device_id_type=MESH)
    pl.semaphore_signal(barrier, inc=1, device_id=(previous, me), device_id_type=MESH)
    pl.semaphore_wait(barrier, T + 1)

    def rows(g):
        return pl.ds(g * R, R)

    def rs_copy(g, k, source):
        return pltpu.make_async_remote_copy(
            src_ref=source, dst_ref=rs.at[g, k], send_sem=rs_send.at[g, k], recv_sem=rs_recv.at[g, k],
            device_id=(sec, sides[side_of[g]]), device_id_type=MESH,
        )

    def shift_copy(g):
        return pltpu.make_async_remote_copy(
            src_ref=hand.at[rows(g)], dst_ref=xb.at[me, rows(g)], send_sem=sh_send.at[g], recv_sem=sh_recv.at[g],
            device_id=(following, me), device_id_type=MESH,
        )

    def ag_copy(g, k, owner):
        return pltpu.make_async_remote_copy(
            src_ref=xb.at[owner, rows(g)], dst_ref=xb.at[owner, rows(g)],
            send_sem=ag_send.at[g, k], recv_sem=ag_recv.at[g, k],
            device_id=(sec, sides[side_of[g]]), device_id_type=MESH,
        )

    def gain_copy(peer, slot):
        return pltpu.make_async_remote_copy(
            src_ref=gain, dst_ref=gains.at[slot], send_sem=g_send.at[peer], recv_sem=g_recv.at[slot],
            device_id=(sec, peer), device_id_type=MESH,
        )

    def kv_copy(peer, slot):
        return pltpu.make_async_remote_copy(
            src_ref=kvall.at[me], dst_ref=kvall.at[slot], send_sem=kv_send.at[peer], recv_sem=kv_recv.at[slot],
            device_id=(sec, peer), device_id_type=MESH,
        )

    def each_peer(act):
        def step(j, c):
            act((me + j) % T)
            return c

        lax.fori_loop(1, T, step, 0)

    def term(side, owner):
        return jnp.dot(
            ctx[pl.ds(side * half, half), :],
            ow[:, pl.ds(pl.multiple_of(owner * B, B), B)],
            preferred_element_type=F32,
        )

    loads[0].wait()
    for side in range(2):
        part = term(side, at(-signs[side])).astype(BF16)
        for g in range(NG):
            if side_of[g] == side:
                start = g * R - side * half
                first[g] = part[start:start + R]
                rs_copy(g, 0, first.at[g]).start()

    gains[me] = gain[...]
    each_peer(lambda peer: gain_copy(peer, me).start())

    loads[1].wait()
    CH = 512

    def place(i, c):
        at_rows = pl.ds(pl.multiple_of(i * CH, CH), CH)
        w[at_rows, HD:] = jnp.concatenate([kvw[at_rows, :], jnp.zeros((CH, HD - KC), BF16)], axis=1)
        return c

    lax.fori_loop(0, D // CH, place, 0)

    def reduce_step(k, c):
        parts = [term(side, at(-signs[side] * (2 + k))) for side in range(2)]
        for j in range(NG // 2):
            for g in (j, j + NG // 2):
                start = j * R
                rs_copy(g, k, first.at[g]).wait_recv()
                rs[g, k] = (rs[g, k].astype(F32) + parts[side_of[g]][start:start + R]).astype(BF16)
                rs_copy(g, k + 1, rs.at[g, k]).start()
        return c

    lax.fori_loop(0, T - 2, reduce_step, 0)

    parts = [term(side, me) for side in range(2)]
    for j in range(NG // 2):
        for g in (j, j + NG // 2):
            rs_copy(g, T - 2, first.at[g]).wait_recv()
            total = rs[g, T - 2].astype(F32) + parts[side_of[g]][j * R:j * R + R]
            hand[rows(g), :] = (res[rows(g), :].astype(F32) + total).astype(BF16)
            shift_copy(g).start()

    for j in range(NG // 2):
        for g in (j, j + NG // 2):
            shift_copy(g).wait_recv()
            ag_copy(g, 0, me).start()

    each_peer(lambda peer: gain_copy(peer, peer).wait_recv())
    loads[2].wait()
    acc[...] = jnp.zeros_like(acc)
    ssq[...] = jnp.zeros_like(ssq)
    ones = jnp.ones((B, HD), BF16)

    def project(side, owner):
        at_rows = pl.ds(side * half, half)
        block = xb[owner, at_rows, :].astype(F32)
        scaled = (block * gains[owner]).astype(BF16)
        squares = (block * block).astype(BF16)
        acc[at_rows, :] += jnp.dot(
            scaled, w[pl.ds(pl.multiple_of(owner * B, B), B), :], preferred_element_type=F32
        )
        ssq[at_rows, :] += jnp.dot(squares, ones, preferred_element_type=F32)

    for side in range(2):
        project(side, me)

    def gather_step(k, c):
        owners = [at(-signs[side] * (1 + k)) for side in range(2)]
        for j in range(NG // 2):
            for g in (j, j + NG // 2):
                ag_copy(g, k, owners[side_of[g]]).wait_recv()
                ag_copy(g, k + 1, owners[side_of[g]]).start()
        for side in range(2):
            project(side, owners[side])
        return c

    lax.fori_loop(0, T - 2, gather_step, 0)
    owners = [at(-signs[side] * (T - 1)) for side in range(2)]
    for j in range(NG // 2):
        for g in (j, j + NG // 2):
            ag_copy(g, T - 2, owners[side_of[g]]).wait_recv()
    for side in range(2):
        project(side, owners[side])

    factor = lax.rsqrt(ssq[...] * (1.0 / D) + EPS)
    pairs = (acc[:, HD:] * factor).astype(BF16)
    picks = lax.broadcasted_iota(jnp.int32, (KC, HD), 0) == lax.broadcasted_iota(jnp.int32, (KC, HD), 1)
    kvall[me] = dot_nt(picks.astype(F32).astype(BF16), pairs).astype(BF16)
    each_peer(lambda peer: kv_copy(peer, me).start())

    queries = acc[:, :HD] * factor
    turned = jnp.concatenate([queries[:, HD // 2:], queries[:, :HD // 2]], axis=1)
    queries = (queries * cos_q[...] + turned * sin_q[...]).astype(BF16)

    share = HD // T
    shift = share.bit_length() - 1
    feature = lax.broadcasted_iota(jnp.int32, (HD, T * KC), 0)
    column = lax.broadcasted_iota(jnp.int32, (HD, T * KC), 1)
    source = (feature >> shift) * KC + (feature & (share - 1)) + (me // GROUP) * (2 * share)
    key_picks = (column == source).astype(F32).astype(BF16)
    value_picks = (column == source + share).astype(F32).astype(BF16)

    each_peer(lambda peer: kv_copy(peer, peer).wait_recv())
    everything = kvall[...].reshape(T * KC, L)
    keys = jnp.dot(key_picks, everything, preferred_element_type=F32)
    values = jnp.dot(value_picks, everything, preferred_element_type=F32).astype(BF16)
    turned = jnp.concatenate([keys[HD // 2:], keys[:HD // 2]], axis=0)
    keys = (keys * cos_k[...] + turned * sin_k[...]).astype(BF16)
    scores = jnp.dot(queries, keys, preferred_element_type=F32) * (HD ** -0.5)
    before = lax.broadcasted_iota(jnp.int32, (L, L), 0) >= lax.broadcasted_iota(jnp.int32, (L, L), 1)
    scores = jnp.where(before, scores, -1e30)
    weights = jnp.exp(scores - jnp.max(scores, axis=1, keepdims=True))
    weights = (weights / jnp.sum(weights, axis=1, keepdims=True)).astype(BF16)
    out[...] = dot_nt(weights, values).astype(BF16)

    def drain(k, c):
        for g in range(NG):
            rs_copy(g, k, first.at[g]).wait_send()
            ag_copy(g, k, me).wait_send()
        return c

    lax.fori_loop(0, T - 1, drain, 0)
    for g in range(NG):
        shift_copy(g).wait_send()
    each_peer(lambda peer: gain_copy(peer, me).wait_send())
    each_peer(lambda peer: kv_copy(peer, me).wait_send())


def on_device(context, out_weight, residual, gain, q_weight, kv_weight):
    T = lax.axis_size("tensor")
    S = lax.axis_size("section")
    _, L, HD = context.shape
    B = residual.shape[2]
    D = out_weight.shape[2]
    KC = kv_weight.shape[2]
    tables = rope_tables(L, HD)
    vmem = pl.BlockSpec(memory_space=pltpu.VMEM)
    anywhere = pl.BlockSpec(memory_space=pl.ANY)
    dma = pltpu.SemaphoreType.DMA
    attended = pl.pallas_call(
        functools.partial(kernel, T, S),
        out_shape=jax.ShapeDtypeStruct((L, HD), BF16),
        in_specs=[vmem] * 7 + [anywhere] * 3,
        out_specs=vmem,
        scratch_shapes=[
            pltpu.VMEM((HD, D), BF16),
            pltpu.VMEM((D, KC), BF16),
            pltpu.VMEM((D, 2 * HD), BF16),
            pltpu.VMEM((NG, L // NG, B), BF16),
            pltpu.VMEM((NG, T - 1, L // NG, B), BF16),
            pltpu.VMEM((L, B), BF16),
            pltpu.VMEM((T, L, B), BF16),
            pltpu.VMEM((T, 1, B), F32),
            pltpu.VMEM((L, 2 * HD), F32),
            pltpu.VMEM((L, HD), F32),
            pltpu.VMEM((T, KC, L), BF16),
            dma((3,)),
            dma((NG, T - 1)), dma((NG, T - 1)),
            dma((NG,)), dma((NG,)),
            dma((NG, T - 1)), dma((NG, T - 1)),
            dma((T,)), dma((T,)),
            dma((T,)), dma((T,)),
        ],
        compiler_params=pltpu.CompilerParams(
            collective_id=0, has_side_effects=True, vmem_limit_bytes=44 * 2**20
        ),
        cost_estimate=pl.CostEstimate(
            flops=2 * L * D * HD * 3, bytes_accessed=D * HD * 6, transcendentals=L * L
        ),
        name="handover_attention",
    )(
        context[0], residual[0], gain, *[jnp.asarray(t) for t in tables],
        out_weight[0], q_weight[0], kv_weight[0],
    )
    return attended[None]


def solution(mesh):
    placed = (
        P("section", None, "tensor"),
        P("section", "tensor", None),
        P("section", None, "tensor"),
        P("section", "tensor"),
        P("section", None, "tensor"),
        P("section", None, "tensor"),
    )
    return jax.shard_map(
        on_device,
        mesh=mesh,
        in_specs=placed,
        out_specs=P("section", None, "tensor"),
        check_vma=False,
    )
```

time: 271 us -> 102 us (0.38)
  waiting for transfers between devices: 183 us -> 0 us
  Pallas kernels: 0 us -> 96.3 us
  blocking collectives: 61 us -> 0 us
  between operations: 13.5 us -> 0.1 us
  matrix products: 8.32 us -> 0 us
  local copies, waits for them, and re-layouts: 1.62 us -> 5.86 us
  other arithmetic: 3.42 us -> 0 us
    pallas_call x0 -> x1, Pallas kernels: none -> 96.3 us  [on_device(): pl.pallas_call(functools.partial(kernel, T, S), out_shape=jax.ShapeDtypeS...]
    reduce_scatter x1 -> x0, waiting for transfers between devices: 91.3 us -> none  [on_device(): lax.psum_scatter(terms.astype(jnp.bfloat16), 'tensor', scatter_dimension=...]
    all_gather x1 -> x0, waiting for transfers between devices: 73.5 us -> none  [on_device(): gathered = lax.all_gather(combined, 'tensor', axis=1, tiled=True)]
    all_gather x2 -> x0, blocking collectives: 61 us -> none  [the longest x1 30.6 us: on_device(): all_pairs = lax.all_gather(pair_part, 'tensor', axis=1, tiled=True)]
    ppermute x1 -> x0, waiting for transfers between devices: 17.7 us -> none  [passed_along(): return lax.ppermute(block, axis, route)]
    dot_general x5 -> x0, matrix products: 8.32 us -> none  [the longest x1 4.01 us: on_device(): jnp.dot(local_context, local_out, preferred_element_type=jnp.float32)]
    unnamed x10 -> x20, local copies, waits for them, and re-layouts: 1.61 us -> 5.86 us
  transfers between devices with their start and end apart: 3 -> 0, of which waited for: 3 -> 0; matrix products, arithmetic and copies ran while one was open for 0% -> 0% of each run, Pallas kernels for 0% -> 0%
where the time goes in v1:
time: 102 us
  Pallas kernels  96.3 us (94%)
  local copies, waits for them, and re-layouts  5.86 us (6%)
    pallas_call x1, Pallas kernels, on_device(): pl.pallas_call(functools.partial(kernel, T, S), out_shape=jax.ShapeDtypeS...  96.3 us
    unnamed x20, local copies, waits for them, and re-layouts  5.86 us

profile of v1, /device:TPU:0, one launch (start us, length us, event | category | flops | bytes accessed | tf_op | source)
XLA Modules:
  0.0 102.3 jit_solution(3292658862167331553)
XLA Ops:
  0.0 0.0 copy-start.3
  0.0 0.0 copy-start.4
  0.0 0.0 copy-start.5
  0.0 0.0 copy-start.6
  0.0 0.0 copy-start.8
  0.0 0.0 copy-start.2
  0.0 0.0 copy-start.7
  0.0 2.0 %copy.11 = bf16[1,8192,32]{2,1,0:T(8,128)(2,1)S(1)} copy(bf16[1,8192,32]{1,2,0:T(8,128)(2,1)} %param.15) | data formatting | bytes 1048576 | tf_op args[5]
  2.1 0.0 copy-done.3
  2.1 0.0 copy-done.4
  2.1 0.0 copy-done.5
  2.1 0.0 copy-done.6
  2.1 0.0 copy-done.8
  2.1 0.0 copy-done.2
  2.1 0.0 copy-done.7
  2.1 0.0 copy-start
  2.1 1.6 %copy-done = bf16[1,128,8192]{2,1,0:T(8,128)(2,1)S(1)} copy-done((bf16[1,128,8192]{2,1,0:T(8,128)(2,1)S(1)}, bf16[1,128,8192]{2,1,0:T(8,128)(2,1)}, u32[]{:S(2)}) %copy-start) | copy-done | bytes 2097176
  3.7 0.0 copy-start.1
  3.7 1.6 %copy-done.1 = bf16[1,8192,128]{2,1,0:T(8,128)(2,1)S(1)} copy-done((bf16[1,8192,128]{2,1,0:T(8,128)(2,1)S(1)}, bf16[1,8192,128]{2,1,0:T(8,128)(2,1)}, u32[]{:S(2)}) %copy-start.1) | copy-done | bytes 2097176
  5.3 96.3 %handover_attention.1 = bf16[256,128]{1,0:T(8,128)(2,1)S(1)} custom-call(bf16[256,128]{1,0:T(8,128)(2,1)S(1)} %bitcast.11, bf16[256,1024]{1,0:T(8,128)(2,1)S(1)} %bitcast.9, f32[1,1024]{1,0:T(1,128)S(1)} %copy-done.8, f32[256,128]{1,0:T(8,128)S(1)} %copy-done.6, f32[256,128]{1,0:T(8,128)S(1)} %copy-done.5, f32[128,256]{1,0:T(8,128)S(1)} %copy-done.4, ...), custom_call_target="tpu_custom_call" | custom-call | flops 1610612736 | bytes 6291456 | tf_op jit(solution)/shard_map/handover_attention/pallas_call | solution.py:275
  101.7 0.6 copy.13
Async XLA Ops:
  0.0 2.1 %copy-start.3 = (f32[128,256]{1,0:T(8,128)S(1)}, f32[128,256]{1,0:T(8,128)}, u32[]{:S(2)}) copy-start(f32[128,256]{1,0:T(8,128)} %constant.11.clone.sin_k) | copy-start | bytes 393220
  0.0 2.1 %copy-start.4 = (f32[128,256]{1,0:T(8,128)S(1)}, f32[128,256]{1,0:T(8,128)}, u32[]{:S(2)}) copy-start(f32[128,256]{1,0:T(8,128)} %constant.10.clone.cos_k) | copy-start | bytes 393220
  0.0 2.1 %copy-start.5 = (f32[256,128]{1,0:T(8,128)S(1)}, f32[256,128]{1,0:T(8,128)}, u32[]{:S(2)}) copy-start(f32[256,128]{1,0:T(8,128)} %constant.9.clone.sin_q) | copy-start | bytes 393220
  0.0 2.1 %copy-start.6 = (f32[256,128]{1,0:T(8,128)S(1)}, f32[256,128]{1,0:T(8,128)}, u32[]{:S(2)}) copy-start(f32[256,128]{1,0:T(8,128)} %constant.8.clone.cos_q) | copy-start | bytes 393220
  0.0 2.1 %copy-start.8 = (f32[1,1024]{1,0:T(1,128)S(1)}, f32[1,1024]{1,0:T(1,128)}, u32[]{:S(2)}) copy-start(f32[1,1024]{1,0:T(1,128)} %gain.1) | copy-start | bytes 12292
  0.0 2.1 %copy-start.2 = (bf16[1,256,1024]{2,1,0:T(8,128)(2,1)S(1)}, bf16[1,256,1024]{2,1,0:T(8,128)(2,1)}, u32[]{:S(2)}) copy-start(bf16[1,256,1024]{2,1,0:T(8,128)(2,1)} %param.12) | copy-start | bytes 1572868
  0.0 2.1 %copy-start.7 = (bf16[1,256,128]{2,1,0:T(8,128)(2,1)S(1)}, bf16[1,256,128]{2,1,0:T(8,128)(2,1)}, u32[]{:S(2)}) copy-start(bf16[1,256,128]{2,1,0:T(8,128)(2,1)} %param.10) | copy-start | bytes 196612
  2.1 1.6 %copy-start = (bf16[1,128,8192]{2,1,0:T(8,128)(2,1)S(1)}, bf16[1,128,8192]{2,1,0:T(8,128)(2,1)}, u32[]{:S(2)}) copy-start(bf16[1,128,8192]{2,1,0:T(8,128)(2,1)} %param.11) | copy-start | bytes 6291460
  3.7 1.6 %copy-start.1 = (bf16[1,8192,128]{2,1,0:T(8,128)(2,1)S(1)}, bf16[1,8192,128]{2,1,0:T(8,128)(2,1)}, u32[]{:S(2)}) copy-start(bf16[1,8192,128]{2,1,0:T(8,128)(2,1)} %param.14) | copy-start | bytes 6291460

commit v2 on v1

v2 whole, which is shorter than its diff:
```python
import functools

import jax
import jax.numpy as jnp
import numpy as np
from jax import lax
from jax.experimental import pallas as pl
from jax.experimental.pallas import tpu as pltpu
from jax.sharding import PartitionSpec as P

GROUP = 8
THETA = 500000.0
EPS = 1e-05
MESH = pl.DeviceIdType.MESH
BF16 = jnp.bfloat16
F32 = jnp.float32
NG = 4
SKEW = 2


def rope_tables(length, head_size):
    half = head_size // 2
    frequency = np.float32(THETA) ** (-(np.arange(half, dtype=np.float32) * np.float32(2.0) / np.float32(head_size)))
    angles = np.arange(length, dtype=np.float32)[:, None] * frequency.astype(np.float32)[None, :]
    cosine, sine = np.cos(angles).astype(np.float32), np.sin(angles).astype(np.float32)
    return (
        np.concatenate([cosine, cosine], axis=1),
        np.concatenate([-sine, sine], axis=1),
        np.ascontiguousarray(np.concatenate([cosine, cosine], axis=1).T),
        np.ascontiguousarray(np.concatenate([-sine, sine], axis=1).T),
    )


def dot_nt(a, b):
    return lax.dot_general(a, b, (((1,), (1,)), ((), ())), preferred_element_type=F32)


def kernel(
    T, S,
    ctx, res, gain, cos_q, sin_q, cos_k, sin_k, ow_hbm, qw_hbm, kvw_hbm,
    out,
    ow, kvw, w, first, rs, hand, xb, gains, acc, ssq, kvall, keys, values,
    ow_sem, load_sem, rs_send, rs_recv, sh_send, sh_recv, ag_send, ag_recv, g_send, g_recv, kv_send, kv_recv,
):
    L, HD = ctx.shape
    B = res.shape[1]
    D = ow.shape[1]
    KC = kvw.shape[0]
    R = L // 4
    half = L // 2
    sec = lax.axis_index("section")
    me = lax.axis_index("tensor")

    def ring(pos):
        upper = pos // (T // 2)
        return (1 - upper) * (2 * pos) + upper * (2 * (T - 1 - pos) + 1)

    y = me % 2
    p = (1 - y) * (me // 2) + y * (T - 1 - me // 2)

    def at(offset):
        return ring((p + offset + 2 * T) % T)

    sides = (at(1), at(-1))
    signs = (1, -1)
    following = (sec + 1) % S
    previous = (sec + S - 1) % S

    def block(owner):
        return pl.ds(pl.multiple_of(owner * B, B), B)

    def ow_copy(owner):
        return pltpu.make_async_copy(ow_hbm.at[:, block(owner)], ow.at[:, block(owner)], ow_sem.at[owner])

    for side in range(2):
        ow_copy(sides[side]).start()

    def load_rest(j, c):
        ow_copy(at(j)).start()
        return c

    def wait_rest(j, c):
        ow_copy(at(j)).wait()
        return c

    lax.fori_loop(2, T - 1, load_rest, 0)
    ow_copy(me).start()
    kv_load = pltpu.make_async_copy(kvw_hbm, kvw, load_sem.at[0])
    kv_load.start()
    q_load = pltpu.make_async_copy(qw_hbm, w.at[:, pl.ds(0, HD)], load_sem.at[1])
    q_load.start()

    barrier = pltpu.get_barrier_semaphore()

    def each_peer(act):
        def step(j, c):
            act((me + j) % T)
            return c

        lax.fori_loop(1, T, step, 0)

    def greet(s, t):
        pl.semaphore_signal(barrier, inc=1, device_id=(s, t), device_id_type=MESH)

    each_peer(lambda peer: greet(sec, peer))
    greet(following, me)
    greet(previous, me)

    def rows(c, side):
        return pl.ds(c * half + side * R, R)

    def rs_copy(c, side, k, source):
        g = 2 * c + side
        return pltpu.make_async_remote_copy(
            src_ref=source, dst_ref=rs.at[g, k], send_sem=rs_send.at[g, k], recv_sem=rs_recv.at[g, k],
            device_id=(sec, sides[side]), device_id_type=MESH,
        )

    def shift_copy(c, side):
        g = 2 * c + side
        return pltpu.make_async_remote_copy(
            src_ref=hand.at[rows(c, side)], dst_ref=xb.at[me, rows(c, side)],
            send_sem=sh_send.at[g], recv_sem=sh_recv.at[g],
            device_id=(following, me), device_id_type=MESH,
        )

    def ag_copy(c, side, k, owner):
        g = 2 * c + side
        return pltpu.make_async_remote_copy(
            src_ref=xb.at[owner, rows(c, side)], dst_ref=xb.at[owner, rows(c, side)],
            send_sem=ag_send.at[g, k], recv_sem=ag_recv.at[g, k],
            device_id=(sec, sides[side]), device_id_type=MESH,
        )

    def gain_copy(peer, slot):
        return pltpu.make_async_remote_copy(
            src_ref=gain, dst_ref=gains.at[slot], send_sem=g_send.at[peer], recv_sem=g_recv.at[slot],
            device_id=(sec, peer), device_id_type=MESH,
        )

    def kv_copy(c, peer, slot):
        columns = pl.ds(c * half, half)
        return pltpu.make_async_remote_copy(
            src_ref=kvall.at[me, :, columns], dst_ref=kvall.at[slot, :, columns],
            send_sem=kv_send.at[c, peer], recv_sem=kv_recv.at[c, slot],
            device_id=(sec, peer), device_id_type=MESH,
        )

    def term(c, side, owner):
        return jnp.dot(ctx[rows(c, side), :], ow[:, block(owner)], preferred_element_type=F32)

    def start_terms(c):
        for side in range(2):
            first[2 * c + side] = term(c, side, at(-signs[side])).astype(BF16)

    def start_sends(c):
        for side in range(2):
            rs_copy(c, side, 0, first.at[2 * c + side]).start()

    def reduce(c, k):
        parts = [term(c, side, at(-signs[side] * (2 + k))) for side in range(2)]
        for side in range(2):
            g = 2 * c + side
            rs_copy(c, side, k, first.at[g]).wait_recv()
            rs[g, k] = (rs[g, k].astype(F32) + parts[side]).astype(BF16)
            rs_copy(c, side, k + 1, rs.at[g, k]).start()

    def hand_over(c):
        parts = [term(c, side, me) + res[rows(c, side), :].astype(F32) for side in range(2)]
        for side in range(2):
            g = 2 * c + side
            rs_copy(c, side, T - 2, first.at[g]).wait_recv()
            hand[rows(c, side), :] = (rs[g, T - 2].astype(F32) + parts[side]).astype(BF16)
            shift_copy(c, side).start()

    def project(c, side, owner):
        features = xb[owner, rows(c, side), :].astype(F32)
        scaled = (features * gains[owner]).astype(BF16)
        squares = features * features
        total = squares[:, :HD]
        for i in range(1, B // HD):
            total = total + squares[:, i * HD:(i + 1) * HD]
        ssq[rows(c, side), :] += total
        acc[rows(c, side), :] += jnp.dot(scaled, w[block(owner), :], preferred_element_type=F32)

    def spread(c):
        for side in range(2):
            shift_copy(c, side).wait_recv()
            ag_copy(c, side, 0, me).start()
        for side in range(2):
            project(c, side, me)

    def pass_on(c, k):
        owners = [at(-signs[side] * (1 + k)) for side in range(2)]
        for side in range(2):
            ag_copy(c, side, k, owners[side]).wait_recv()
            ag_copy(c, side, k + 1, owners[side]).start()
        for side in range(2):
            project(c, side, owners[side])

    def arrive(c):
        owners = [at(-signs[side] * (T - 1)) for side in range(2)]
        for side in range(2):
            ag_copy(c, side, T - 2, owners[side]).wait_recv()
            project(c, side, owners[side])

    def place(i):
        w[block(i), HD:] = jnp.concatenate(
            [jnp.transpose(kvw[:, block(i)]), jnp.zeros((B, HD - KC), BF16)], axis=1
        )

    for side in range(2):
        ow_copy(sides[side]).wait()
    start_terms(0)
    pl.semaphore_wait(barrier, T + 1)
    start_sends(0)

    gains[me] = gain[...]
    each_peer(lambda peer: gain_copy(peer, me).start())
    start_terms(1)
    acc[...] = jnp.zeros_like(acc)
    ssq[...] = jnp.zeros_like(ssq)
    lax.fori_loop(2, T - 1, wait_rest, 0)
    ow_copy(me).wait()
    kv_load.wait()
    place(T - 2)
    place(T - 1)
    each_peer(lambda peer: gain_copy(peer, peer).wait_recv())
    q_load.wait()

    def slot(j, c):
        for cls in range(2):
            i = j - SKEW * cls
            if cls:
                pl.when(i == -1)(lambda: start_sends(1))
            pl.when((i >= 0) & (i < T - 2))(functools.partial(reduce, cls, i))
            pl.when(i == T - 2)(functools.partial(hand_over, cls))
            pl.when(i == T - 1)(functools.partial(spread, cls))
            pl.when((i >= T) & (i < 2 * T - 2))(functools.partial(pass_on, cls, i - T))
        pl.when(j < T - 2)(functools.partial(place, j))
        return c

    lax.fori_loop(0, 2 * T - 2, slot, 0)

    share = HD // T
    shift = share.bit_length() - 1
    feature = lax.broadcasted_iota(jnp.int32, (HD, T * KC), 0)
    column = lax.broadcasted_iota(jnp.int32, (HD, T * KC), 1)
    source = (feature >> shift) * KC + (feature & (share - 1)) + (me // GROUP) * (2 * share)
    key_picks = (column == source).astype(F32).astype(BF16)
    value_picks = (column == source + share).astype(F32).astype(BF16)
    eye = lax.broadcasted_iota(jnp.int32, (KC, HD), 0) == lax.broadcasted_iota(jnp.int32, (KC, HD), 1)
    eye = eye.astype(F32).astype(BF16)

    def finish(c):
        part = pl.ds(c * half, half)
        factor = lax.rsqrt(jnp.sum(ssq[part, :], axis=1, keepdims=True) * (1.0 / D) + EPS)
        pairs = (acc[part, HD:] * factor).astype(BF16)
        kvall[me, :, part] = dot_nt(eye, pairs).astype(BF16)
        each_peer(lambda peer: kv_copy(c, peer, me).start())
        queries = acc[part, :HD] * factor
        turned = jnp.concatenate([queries[:, HD // 2:], queries[:, :HD // 2]], axis=1)
        return (queries * cos_q[part, :] + turned * sin_q[part, :]).astype(BF16)

    def attend(c, queries):
        part = pl.ds(c * half, half)
        each_peer(lambda peer: kv_copy(c, peer, peer).wait_recv())
        everything = kvall[:, :, part].reshape(T * KC, half)
        found = jnp.dot(key_picks, everything, preferred_element_type=F32)
        turned = jnp.concatenate([found[HD // 2:], found[:HD // 2]], axis=0)
        keys[:, part] = (found * cos_k[:, part] + turned * sin_k[:, part]).astype(BF16)
        values[:, part] = jnp.dot(value_picks, everything, preferred_element_type=F32).astype(BF16)
        seen = (c + 1) * half
        scores = jnp.dot(queries, keys[:, :seen], preferred_element_type=F32) * (HD ** -0.5)
        before = lax.broadcasted_iota(jnp.int32, (half, seen), 0) + c * half >= lax.broadcasted_iota(
            jnp.int32, (half, seen), 1
        )
        scores = jnp.where(before, scores, -1e30)
        weights = jnp.exp(scores - jnp.max(scores, axis=1, keepdims=True))
        weights = (weights / jnp.sum(weights, axis=1, keepdims=True)).astype(BF16)
        out[part, :] = dot_nt(weights, values[:, :seen]).astype(BF16)

    arrive(0)
    pass_on(1, T - 2 - SKEW)
    queries = finish(0)

    def late(k, c):
        pass_on(1, k)
        return c

    lax.fori_loop(T - 1 - SKEW, T - 2, late, 0)
    attend(0, queries)
    arrive(1)
    attend(1, finish(1))

    def drain(k, c):
        for cls in range(2):
            for side in range(2):
                rs_copy(cls, side, k, first.at[0]).wait_send()
                ag_copy(cls, side, k, me).wait_send()
        return c

    lax.fori_loop(0, T - 1, drain, 0)
    for cls in range(2):
        for side in range(2):
            shift_copy(cls, side).wait_send()
        each_peer(lambda peer: kv_copy(cls, peer, me).wait_send())
    each_peer(lambda peer: gain_copy(peer, me).wait_send())


def on_device(context, out_weight, residual, gain, q_weight, kv_weight):
    T = lax.axis_size("tensor")
    S = lax.axis_size("section")
    _, L, HD = context.shape
    B = residual.shape[2]
    D = out_weight.shape[2]
    KC = kv_weight.shape[2]
    tables = rope_tables(L, HD)
    vmem = pl.BlockSpec(memory_space=pltpu.VMEM)
    anywhere = pl.BlockSpec(memory_space=pl.ANY)
    dma = pltpu.SemaphoreType.DMA
    attended = pl.pallas_call(
        functools.partial(kernel, T, S),
        out_shape=jax.ShapeDtypeStruct((L, HD), BF16),
        in_specs=[vmem] * 7 + [anywhere] * 3,
        out_specs=vmem,
        scratch_shapes=[
            pltpu.VMEM((HD, D), BF16),
            pltpu.VMEM((KC, D), BF16),
            pltpu.VMEM((D, 2 * HD), BF16),
            pltpu.VMEM((NG, L // NG, B), BF16),
            pltpu.VMEM((NG, T - 1, L // NG, B), BF16),
            pltpu.VMEM((L, B), BF16),
            pltpu.VMEM((T, L, B), BF16),
            pltpu.VMEM((T, 1, B), F32),
            pltpu.VMEM((L, 2 * HD), F32),
            pltpu.VMEM((L, HD), F32),
            pltpu.VMEM((T, KC, L), BF16),
            pltpu.VMEM((HD, L), BF16),
            pltpu.VMEM((HD, L), BF16),
            dma((T,)), dma((2,)),
            dma((NG, T - 1)), dma((NG, T - 1)),
            dma((NG,)), dma((NG,)),
            dma((NG, T - 1)), dma((NG, T - 1)),
            dma((T,)), dma((T,)),
            dma((2, T)), dma((2, T)),
        ],
        compiler_params=pltpu.CompilerParams(
            collective_id=0, has_side_effects=True, vmem_limit_bytes=62 * 2**20
        ),
        cost_estimate=pl.CostEstimate(
            flops=2 * L * D * HD * 3, bytes_accessed=D * HD * 6, transcendentals=L * L
        ),
        name="handover_attention",
    )(
        context[0], residual[0], gain, *[jnp.asarray(t) for t in tables],
        out_weight[0], q_weight[0], jnp.swapaxes(kv_weight[0], 0, 1),
    )
    return attended[None]


def solution(mesh):
    placed = (
        P("section", None, "tensor"),
        P("section", "tensor", None),
        P("section", None, "tensor"),
        P("section", "tensor"),
        P("section", None, "tensor"),
        P("section", None, "tensor"),
    )
    return jax.shard_map(
        on_device,
        mesh=mesh,
        in_specs=placed,
        out_specs=P("section", None, "tensor"),
        check_vma=False,
    )
```

time: 102 us -> 109 us (1.069)
  Pallas kernels: 96.3 us -> 107 us
  local copies, waits for them, and re-layouts: 5.86 us -> 1.47 us
    pallas_call x1, Pallas kernels: 96.3 us -> 107 us  [on_device(): pl.pallas_call(functools.partial(kernel, T, S), out_shape=jax.ShapeDtypeS...]
    unnamed x20 -> x1, local copies, waits for them, and re-layouts: 5.86 us -> 1.47 us
where the time goes in v2:
time: 109 us
  Pallas kernels  107 us (98%)
  local copies, waits for them, and re-layouts  1.47 us (1%)
    pallas_call x1, Pallas kernels, on_device(): pl.pallas_call(functools.partial(kernel, T, S), out_shape=jax.ShapeDtypeS...  107 us

profile of v2, /device:TPU:0, one launch (start us, length us, event | category | flops | bytes accessed | tf_op | source)
XLA Modules:
  0.0 108.5 jit_solution(6431407586974118570)
XLA Ops:
  0.0 107.1 %handover_attention.1 = bf16[256,128]{1,0:T(8,128)(2,1)} custom-call(bf16[256,128]{1,0:T(8,128)(2,1)} %bitcast.13, bf16[256,1024]{1,0:T(8,128)(2,1)} %bitcast.11, f32[1,1024]{1,0:T(1,128)} %gain.1, f32[256,128]{1,0:T(8,128)} %constant.8.clone.cos_q, f32[256,128]{1,0:T(8,128)} %constant.9.clone.sin_q, f32[128,256]{1,0:T(8,128)} %constant.10.clone.cos_k, ...), custom_call_target="tpu_custom_call" | custom-call | flops 1610612736 | bytes 6291456 | tf_op jit(solution)/shard_map/handover_attention/pallas_call | solution.py:322
  107.1 1.5 %copy.12 = bf16[1,256,128]{2,1,0:T(8,128)(2,1)} copy(bf16[1,256,128]{2,1,0:T(8,128)(2,1)} %bitcast.8) | data formatting | bytes 131072

commit v3 on v1

v3 whole, which is shorter than its diff:
```python
import functools

import jax
import jax.numpy as jnp
import numpy as np
from jax import lax
from jax.experimental import pallas as pl
from jax.experimental.pallas import tpu as pltpu
from jax.sharding import PartitionSpec as P

GROUP = 8
THETA = 500000.0
EPS = 1e-05
MESH = pl.DeviceIdType.MESH
BF16 = jnp.bfloat16
F32 = jnp.float32
NG = 8


def rope_tables(length, head_size):
    half = head_size // 2
    frequency = np.float32(THETA) ** (-(np.arange(half, dtype=np.float32) * np.float32(2.0) / np.float32(head_size)))
    angles = np.arange(length, dtype=np.float32)[:, None] * frequency.astype(np.float32)[None, :]
    cosine, sine = np.cos(angles).astype(np.float32), np.sin(angles).astype(np.float32)
    return (
        np.concatenate([cosine, cosine], axis=1),
        np.concatenate([-sine, sine], axis=1),
        np.ascontiguousarray(np.concatenate([cosine, cosine], axis=1).T),
        np.ascontiguousarray(np.concatenate([-sine, sine], axis=1).T),
    )


def dot_nt(a, b):
    return lax.dot_general(a, b, (((1,), (1,)), ((), ())), preferred_element_type=F32)


def kernel(
    T, S,
    ctx, res, gain, cos_q, sin_q, cos_k, sin_k, ow_hbm, qw_hbm, kvw_hbm,
    out,
    ow, kvw, w, first, rs, hand, xb, gains, acc, ssq, kvall, terms,
    ow_sem, load_sem, rs_send, rs_recv, sh_send, sh_recv, ag_send, ag_recv, g_send, g_recv, kv_send, kv_recv,
):
    L, HD = ctx.shape
    B = res.shape[1]
    D = ow.shape[1]
    KC = kvw.shape[0]
    R = L // NG
    per_side = NG // 2
    half = L // 2
    sec = lax.axis_index("section")
    me = lax.axis_index("tensor")

    def ring(pos):
        upper = pos // (T // 2)
        return (1 - upper) * (2 * pos) + upper * (2 * (T - 1 - pos) + 1)

    y = me % 2
    p = (1 - y) * (me // 2) + y * (T - 1 - me // 2)

    def at(offset):
        return ring((p + offset + 2 * T) % T)

    sides = (at(1), at(-1))
    signs = (1, -1)
    following = (sec + 1) % S
    previous = (sec + S - 1) % S

    def block(owner):
        return pl.ds(pl.multiple_of(owner * B, B), B)

    def ow_copy(owner):
        return pltpu.make_async_copy(ow_hbm.at[:, block(owner)], ow.at[:, block(owner)], ow_sem.at[owner])

    for side in range(2):
        ow_copy(sides[side]).start()

    def load_rest(j, c):
        ow_copy(at(j)).start()
        return c

    def wait_rest(j, c):
        ow_copy(at(j)).wait()
        return c

    lax.fori_loop(2, T - 1, load_rest, 0)
    ow_copy(me).start()
    kv_load = pltpu.make_async_copy(kvw_hbm, kvw, load_sem.at[0])
    kv_load.start()
    q_load = pltpu.make_async_copy(qw_hbm, w.at[:, pl.ds(0, HD)], load_sem.at[1])
    q_load.start()

    barrier = pltpu.get_barrier_semaphore()

    def each_peer(act):
        def step(j, c):
            act((me + j) % T)
            return c

        lax.fori_loop(1, T, step, 0)

    def greet(s, t):
        pl.semaphore_signal(barrier, inc=1, device_id=(s, t), device_id_type=MESH)

    each_peer(lambda peer: greet(sec, peer))
    greet(following, me)
    greet(previous, me)

    def rows(g):
        return pl.ds(g * R, R)

    def side_of(g):
        return g // per_side

    order = [side * per_side + j for j in range(per_side) for side in range(2)]

    def rs_copy(g, k, source):
        return pltpu.make_async_remote_copy(
            src_ref=source, dst_ref=rs.at[g, k], send_sem=rs_send.at[g, k], recv_sem=rs_recv.at[g, k],
            device_id=(sec, sides[side_of(g)]), device_id_type=MESH,
        )

    def shift_copy(g):
        return pltpu.make_async_remote_copy(
            src_ref=hand.at[rows(g)], dst_ref=xb.at[me, rows(g)], send_sem=sh_send.at[g], recv_sem=sh_recv.at[g],
            device_id=(following, me), device_id_type=MESH,
        )

    def ag_copy(g, k, owner):
        return pltpu.make_async_remote_copy(
            src_ref=xb.at[owner, rows(g)], dst_ref=xb.at[owner, rows(g)],
            send_sem=ag_send.at[g, k], recv_sem=ag_recv.at[g, k],
            device_id=(sec, sides[side_of(g)]), device_id_type=MESH,
        )

    def gain_copy(peer, slot):
        return pltpu.make_async_remote_copy(
            src_ref=gain, dst_ref=gains.at[slot], send_sem=g_send.at[peer], recv_sem=g_recv.at[slot],
            device_id=(sec, peer), device_id_type=MESH,
        )

    def kv_copy(peer, slot):
        return pltpu.make_async_remote_copy(
            src_ref=kvall.at[me], dst_ref=kvall.at[slot], send_sem=kv_send.at[peer], recv_sem=kv_recv.at[slot],
            device_id=(sec, peer), device_id_type=MESH,
        )

    def half_rows(side):
        return pl.ds(side * half, half)

    def set_terms(side, owner):
        terms[half_rows(side), :] = jnp.dot(
            ctx[half_rows(side), :], ow[:, block(owner)], preferred_element_type=F32
        )

    def project(side, owner):
        features = xb[owner, half_rows(side), :].astype(F32)
        scaled = (features * gains[owner]).astype(BF16)
        squares = features * features
        total = squares[:, :HD]
        for i in range(1, B // HD):
            total = total + squares[:, i * HD:(i + 1) * HD]
        ssq[half_rows(side), :] += total
        acc[half_rows(side), :] += jnp.dot(scaled, w[block(owner), :], preferred_element_type=F32)

    def place(i):
        w[block(i), HD:] = jnp.concatenate(
            [jnp.transpose(kvw[:, block(i)]), jnp.zeros((B, HD - KC), BF16)], axis=1
        )

    for side in range(2):
        ow_copy(sides[1 - side]).wait()
        first[half_rows(side), :] = jnp.dot(
            ctx[half_rows(side), :], ow[:, block(sides[1 - side])], preferred_element_type=F32
        ).astype(BF16)
    pl.semaphore_wait(barrier, T + 1)
    for g in order:
        rs_copy(g, 0, first.at[rows(g)]).start()

    lax.fori_loop(2, T - 1, wait_rest, 0)
    ow_copy(me).wait()
    for side in range(2):
        set_terms(side, at(-2 * signs[side]))
    gains[me] = gain[...]
    each_peer(lambda peer: gain_copy(peer, me).start())
    acc[...] = jnp.zeros_like(acc)
    ssq[...] = jnp.zeros_like(ssq)
    kv_load.wait()
    place(T - 2)
    place(T - 1)

    def reduce_step(k, c):
        for g in order:
            rs_copy(g, k, first.at[rows(g)]).wait_recv()
            rs[g, k] = (rs[g, k].astype(F32) + terms[rows(g), :]).astype(BF16)
            rs_copy(g, k + 1, rs.at[g, k]).start()
        for side in range(2):
            set_terms(side, at(-signs[side] * (3 + k)))
        place(k)
        return c

    lax.fori_loop(0, T - 2, reduce_step, 0)

    for g in order:
        rs_copy(g, T - 2, first.at[rows(g)]).wait_recv()
        total = rs[g, T - 2].astype(F32) + terms[rows(g), :]
        hand[rows(g), :] = (res[rows(g), :].astype(F32) + total).astype(BF16)
        shift_copy(g).start()

    each_peer(lambda peer: gain_copy(peer, peer).wait_recv())
    q_load.wait()
    for g in order:
        shift_copy(g).wait_recv()
        ag_copy(g, 0, me).start()
    for side in range(2):
        project(side, me)

    def gather_step(k, c):
        owners = [at(-signs[side] * (1 + k)) for side in range(2)]
        for g in order:
            ag_copy(g, k, owners[side_of(g)]).wait_recv()
            ag_copy(g, k + 1, owners[side_of(g)]).start()
        for side in range(2):
            project(side, owners[side])
        return c

    lax.fori_loop(0, T - 2, gather_step, 0)
    for g in order:
        ag_copy(g, T - 2, at(-signs[side_of(g)] * (T - 1))).wait_recv()
    for side in range(2):
        project(side, at(-signs[side] * (T - 1)))

    factor = lax.rsqrt(jnp.sum(ssq[...], axis=1, keepdims=True) * (1.0 / D) + EPS)
    pairs = (acc[:, HD:] * factor).astype(BF16)
    eye = lax.broadcasted_iota(jnp.int32, (KC, HD), 0) == lax.broadcasted_iota(jnp.int32, (KC, HD), 1)
    kvall[me] = dot_nt(eye.astype(F32).astype(BF16), pairs).astype(BF16)
    each_peer(lambda peer: kv_copy(peer, me).start())

    queries = acc[:, :HD] * factor
    turned = jnp.concatenate([queries[:, HD // 2:], queries[:, :HD // 2]], axis=1)
    queries = (queries * cos_q[...] + turned * sin_q[...]).astype(BF16)

    share = HD // T
    shift = share.bit_length() - 1
    feature = lax.broadcasted_iota(jnp.int32, (HD, T * KC), 0)
    column = lax.broadcasted_iota(jnp.int32, (HD, T * KC), 1)
    source = (feature >> shift) * KC + (feature & (share - 1)) + (me // GROUP) * (2 * share)
    key_picks = (column == source).astype(F32).astype(BF16)
    value_picks = (column == source + share).astype(F32).astype(BF16)

    each_peer(lambda peer: kv_copy(peer, peer).wait_recv())
    everything = kvall[...].reshape(T * KC, L)
    keys = jnp.dot(key_picks, everything, preferred_element_type=F32)
    values = jnp.dot(value_picks, everything, preferred_element_type=F32).astype(BF16)
    turned = jnp.concatenate([keys[HD // 2:], keys[:HD // 2]], axis=0)
    keys = (keys * cos_k[...] + turned * sin_k[...]).astype(BF16)
    for c in range(2):
        seen = (c + 1) * half
        scores = jnp.dot(queries[c * half:seen], keys[:, :seen], preferred_element_type=F32) * (HD ** -0.5)
        before = lax.broadcasted_iota(jnp.int32, (half, seen), 0) + c * half >= lax.broadcasted_iota(
            jnp.int32, (half, seen), 1
        )
        scores = jnp.where(before, scores, -1e30)
        weights = jnp.exp(scores - jnp.max(scores, axis=1, keepdims=True))
        weights = (weights * (1.0 / jnp.sum(weights, axis=1, keepdims=True))).astype(BF16)
        out[half_rows(c), :] = dot_nt(weights, values[:, :seen]).astype(BF16)

    def drain(k, c):
        for g in range(NG):
            rs_copy(g, k, first.at[rows(g)]).wait_send()
            ag_copy(g, k, me).wait_send()
        return c

    lax.fori_loop(0, T - 1, drain, 0)
    for g in range(NG):
        shift_copy(g).wait_send()
    each_peer(lambda peer: gain_copy(peer, me).wait_send())
    each_peer(lambda peer: kv_copy(peer, me).wait_send())


def on_device(context, out_weight, residual, gain, q_weight, kv_weight):
    T = lax.axis_size("tensor")
    S = lax.axis_size("section")
    _, L, HD = context.shape
    B = residual.shape[2]
    D = out_weight.shape[2]
    KC = kv_weight.shape[2]
    tables = rope_tables(L, HD)
    vmem = pl.BlockSpec(memory_space=pltpu.VMEM)
    anywhere = pl.BlockSpec(memory_space=pl.ANY)
    dma = pltpu.SemaphoreType.DMA
    attended = pl.pallas_call(
        functools.partial(kernel, T, S),
        out_shape=jax.ShapeDtypeStruct((L, HD), BF16),
        in_specs=[vmem] * 7 + [anywhere] * 3,
        out_specs=vmem,
        scratch_shapes=[
            pltpu.VMEM((HD, D), BF16),
            pltpu.VMEM((KC, D), BF16),
            pltpu.VMEM((D, 2 * HD), BF16),
            pltpu.VMEM((L, B), BF16),
            pltpu.VMEM((NG, T - 1, L // NG, B), BF16),
            pltpu.VMEM((L, B), BF16),
            pltpu.VMEM((T, L, B), BF16),
            pltpu.VMEM((T, 1, B), F32),
            pltpu.VMEM((L, 2 * HD), F32),
            pltpu.VMEM((L, HD), F32),
            pltpu.VMEM((T, KC, L), BF16),
            pltpu.VMEM((L, B), F32),
            dma((T,)), dma((2,)),
            dma((NG, T - 1)), dma((NG, T - 1)),
            dma((NG,)), dma((NG,)),
            dma((NG, T - 1)), dma((NG, T - 1)),
            dma((T,)), dma((T,)),
            dma((T,)), dma((T,)),
        ],
        compiler_params=pltpu.CompilerParams(
            collective_id=0, has_side_effects=True, vmem_limit_bytes=62 * 2**20
        ),
        cost_estimate=pl.CostEstimate(
            flops=2 * L * D * HD * 3, bytes_accessed=D * HD * 6, transcendentals=L * L
        ),
        name="handover_attention",
    )(
        context[0], residual[0], gain, *[jnp.asarray(t) for t in tables],
        out_weight[0], q_weight[0], jnp.swapaxes(kv_weight[0], 0, 1),
    )
    return attended[None]


def solution(mesh):
    placed = (
        P("section", None, "tensor"),
        P("section", "tensor", None),
        P("section", None, "tensor"),
        P("section", "tensor"),
        P("section", None, "tensor"),
        P("section", None, "tensor"),
    )
    return jax.shard_map(
        on_device,
        mesh=mesh,
        in_specs=placed,
        out_specs=P("section", None, "tensor"),
        check_vma=False,
    )
```

time: 102 us -> 99.5 us (0.975)
  local copies, waits for them, and re-layouts: 5.86 us -> 1.47 us
  Pallas kernels: 96.3 us -> 97.8 us
    unnamed x20 -> x1, local copies, waits for them, and re-layouts: 5.86 us -> 1.47 us
    pallas_call x1, Pallas kernels: 96.3 us -> 97.8 us  [on_device(): pl.pallas_call(functools.partial(kernel, T, S), out_shape=jax.ShapeDtypeS...]
where the time goes in v3:
time: 99.5 us; the launch traced here: 99.3 us
  Pallas kernels  97.8 us (98%)
  local copies, waits for them, and re-layouts  1.47 us (1%)
    pallas_call x1, Pallas kernels, on_device(): pl.pallas_call(functools.partial(kernel, T, S), out_shape=jax.ShapeDtypeS...  97.8 us

profile of v3, /device:TPU:0, one launch (start us, length us, event | category | flops | bytes accessed | tf_op | source)
XLA Modules:
  0.0 99.3 jit_solution(16191177064185225574)
XLA Ops:
  0.0 97.8 %handover_attention.1 = bf16[256,128]{1,0:T(8,128)(2,1)} custom-call(bf16[256,128]{1,0:T(8,128)(2,1)} %bitcast.13, bf16[256,1024]{1,0:T(8,128)(2,1)} %bitcast.11, f32[1,1024]{1,0:T(1,128)} %gain.1, f32[256,128]{1,0:T(8,128)} %constant.8.clone.cos_q, f32[256,128]{1,0:T(8,128)} %constant.9.clone.sin_q, f32[128,256]{1,0:T(8,128)} %constant.10.clone.cos_k, ...), custom_call_target="tpu_custom_call" | custom-call | flops 1610612736 | bytes 6291456 | tf_op jit(solution)/shard_map/handover_attention/pallas_call | solution.py:292
  97.8 1.5 %copy.12 = bf16[1,256,128]{2,1,0:T(8,128)(2,1)} copy(bf16[1,256,128]{2,1,0:T(8,128)(2,1)} %bitcast.8) | data formatting | bytes 131072

commit v4 on v3

--- a/solution.py
+++ b/solution.py
@@ -14,7 +14,7 @@
 MESH = pl.DeviceIdType.MESH
 BF16 = jnp.bfloat16
 F32 = jnp.float32
-NG = 8
+NG = 4
 
 
 def rope_tables(length, head_size):
@@ -46,7 +46,7 @@
     D = ow.shape[1]
     KC = kvw.shape[0]
     R = L // NG
-    per_side = NG // 2
+    H = T // 2
     half = L // 2
     sec = lax.axis_index("section")
     me = lax.axis_index("tensor")
@@ -72,8 +72,9 @@
     def ow_copy(owner):
         return pltpu.make_async_copy(ow_hbm.at[:, block(owner)], ow.at[:, block(owner)], ow_sem.at[owner])
 
-    for side in range(2):
-        ow_copy(sides[side]).start()
+    ow_copy(at(H)).start()
+    ow_copy(at(H - 1)).start()
+    ow_copy(at(1 - H)).start()
 
     def load_rest(j, c):
         ow_copy(at(j)).start()
@@ -83,8 +84,7 @@
         ow_copy(at(j)).wait()
         return c
 
-    lax.fori_loop(2, T - 1, load_rest, 0)
-    ow_copy(me).start()
+    lax.fori_loop(T + 2 - H, T + H - 1, load_rest, 0)
     kv_load = pltpu.make_async_copy(kvw_hbm, kvw, load_sem.at[0])
     kv_load.start()
     q_load = pltpu.make_async_copy(qw_hbm, w.at[:, pl.ds(0, HD)], load_sem.at[1])
@@ -109,15 +109,17 @@
     def rows(g):
         return pl.ds(g * R, R)
 
-    def side_of(g):
-        return g // per_side
-
-    order = [side * per_side + j for j in range(per_side) for side in range(2)]
-
-    def rs_copy(g, k, source):
-        return pltpu.make_async_remote_copy(
-            src_ref=source, dst_ref=rs.at[g, k], send_sem=rs_send.at[g, k], recv_sem=rs_recv.at[g, k],
-            device_id=(sec, sides[side_of(g)]), device_id_type=MESH,
+    def is_long(side, g):
+        return (g // (NG // 2)) == side
+
+    order = [g for j in range(NG // 2) for g in (j, j + NG // 2)]
+    pairs_of = [(side, g) for g in order for side in range(2)]
+
+    def rs_copy(side, g, left, source):
+        return pltpu.make_async_remote_copy(
+            src_ref=source, dst_ref=rs.at[side, left - 1, rows(g)],
+            send_sem=rs_send.at[side, g, left - 1], recv_sem=rs_recv.at[side, g, left - 1],
+            device_id=(sec, sides[side]), device_id_type=MESH,
         )
 
     def shift_copy(g):
@@ -126,11 +128,11 @@
             device_id=(following, me), device_id_type=MESH,
         )
 
-    def ag_copy(g, k, owner):
+    def ag_copy(side, g, k, owner):
         return pltpu.make_async_remote_copy(
             src_ref=xb.at[owner, rows(g)], dst_ref=xb.at[owner, rows(g)],
-            send_sem=ag_send.at[g, k], recv_sem=ag_recv.at[g, k],
-            device_id=(sec, sides[side_of(g)]), device_id_type=MESH,
+            send_sem=ag_send.at[side, g, k], recv_sem=ag_recv.at[side, g, k],
+            device_id=(sec, sides[side]), device_id_type=MESH,
         )
 
     def gain_copy(peer, slot):
@@ -148,87 +150,112 @@
     def half_rows(side):
         return pl.ds(side * half, half)
 
-    def set_terms(side, owner):
-        terms[half_rows(side), :] = jnp.dot(
-            ctx[half_rows(side), :], ow[:, block(owner)], preferred_element_type=F32
-        )
-
-    def project(side, owner):
-        features = xb[owner, half_rows(side), :].astype(F32)
+    def term(owner):
+        return jnp.dot(ctx[...], ow[:, block(owner)], preferred_element_type=F32)
+
+    def project(owner):
+        features = xb[owner].astype(F32)
         scaled = (features * gains[owner]).astype(BF16)
         squares = features * features
         total = squares[:, :HD]
         for i in range(1, B // HD):
             total = total + squares[:, i * HD:(i + 1) * HD]
-        ssq[half_rows(side), :] += total
-        acc[half_rows(side), :] += jnp.dot(scaled, w[block(owner), :], preferred_element_type=F32)
+        ssq[...] += total
+        acc[...] += jnp.dot(scaled, w[block(owner), :], preferred_element_type=F32)
 
     def place(i):
         w[block(i), HD:] = jnp.concatenate(
             [jnp.transpose(kvw[:, block(i)]), jnp.zeros((B, HD - KC), BF16)], axis=1
         )
 
+    ow_copy(at(H)).wait()
+    first[...] = term(at(H)).astype(BF16)
+    pl.semaphore_wait(barrier, T + 1)
+    for side, g in pairs_of:
+        if is_long(side, g):
+            rs_copy(side, g, H, first.at[rows(g)]).start()
+
     for side in range(2):
-        ow_copy(sides[1 - side]).wait()
-        first[half_rows(side), :] = jnp.dot(
-            ctx[half_rows(side), :], ow[:, block(sides[1 - side])], preferred_element_type=F32
-        ).astype(BF16)
-    pl.semaphore_wait(barrier, T + 1)
-    for g in order:
-        rs_copy(g, 0, first.at[rows(g)]).start()
-
-    lax.fori_loop(2, T - 1, wait_rest, 0)
-    ow_copy(me).wait()
-    for side in range(2):
-        set_terms(side, at(-2 * signs[side]))
+        ow_copy(at(signs[side] * (H - 1))).wait()
+        terms[side] = term(at(signs[side] * (H - 1)))
+    for side, g in pairs_of:
+        if not is_long(side, g):
+            rs[side, H - 1, rows(g), :] = terms[side, rows(g), :].astype(BF16)
+            rs_copy(side, g, H - 1, rs.at[side, H - 1, rows(g)]).start()
     gains[me] = gain[...]
     each_peer(lambda peer: gain_copy(peer, me).start())
+
+    for side, g in pairs_of:
+        if is_long(side, g):
+            rs_copy(side, g, H, first.at[rows(g)]).wait_recv()
+            total = rs[side, H - 1, rows(g), :].astype(F32) + terms[side, rows(g), :]
+            rs[side, H - 1, rows(g), :] = total.astype(BF16)
+            rs_copy(side, g, H - 1, rs.at[side, H - 1, rows(g)]).start()
+
+    lax.fori_loop(T + 2 - H, T + H - 1, wait_rest, 0)
+    for side in range(2):
+        terms[side] = term(at(signs[side] * (H - 2)))
     acc[...] = jnp.zeros_like(acc)
     ssq[...] = jnp.zeros_like(ssq)
     kv_load.wait()
     place(T - 2)
     place(T - 1)
 
-    def reduce_step(k, c):
-        for g in order:
-            rs_copy(g, k, first.at[rows(g)]).wait_recv()
-            rs[g, k] = (rs[g, k].astype(F32) + terms[rows(g), :]).astype(BF16)
-            rs_copy(g, k + 1, rs.at[g, k]).start()
+    def reduce_step(i, c):
+        left = H - 2 - i
+        for side, g in pairs_of:
+            rs_copy(side, g, left + 1, first.at[rows(g)]).wait_recv()
+            total = rs[side, left, rows(g), :].astype(F32) + terms[side, rows(g), :]
+            rs[side, left, rows(g), :] = total.astype(BF16)
+            rs_copy(side, g, left, rs.at[side, left, rows(g)]).start()
         for side in range(2):
-            set_terms(side, at(-signs[side] * (3 + k)))
-        place(k)
-        return c
-
-    lax.fori_loop(0, T - 2, reduce_step, 0)
-
+            terms[side] = term(at(signs[side] * (left - 1)))
+        for n in range(2):
+            place(2 * i + n)
+        return c
+
+    lax.fori_loop(0, H - 2, reduce_step, 0)
+    terms[0] += res[...].astype(F32)
     for g in order:
-        rs_copy(g, T - 2, first.at[rows(g)]).wait_recv()
-        total = rs[g, T - 2].astype(F32) + terms[rows(g), :]
-        hand[rows(g), :] = (res[rows(g), :].astype(F32) + total).astype(BF16)
+        for side in range(2):
+            rs_copy(side, g, 1, first.at[rows(g)]).wait_recv()
+        total = rs[0, 0, rows(g), :].astype(F32) + rs[1, 0, rows(g), :].astype(F32) + terms[0, rows(g), :]
+        hand[rows(g), :] = total.astype(BF16)
         shift_copy(g).start()
+    place(T - 4)
+    place(T - 3)
 
     each_peer(lambda peer: gain_copy(peer, peer).wait_recv())
     q_load.wait()
     for g in order:
         shift_copy(g).wait_recv()
-        ag_copy(g, 0, me).start()
-    for side in range(2):
-        project(side, me)
+        for side in range(2):
+            ag_copy(side, g, 0, me).start()
+    project(me)
 
     def gather_step(k, c):
         owners = [at(-signs[side] * (1 + k)) for side in range(2)]
-        for g in order:
-            ag_copy(g, k, owners[side_of(g)]).wait_recv()
-            ag_copy(g, k + 1, owners[side_of(g)]).start()
+        for side, g in pairs_of:
+            ag_copy(side, g, k, owners[side]).wait_recv()
+            ag_copy(side, g, k + 1, owners[side]).start()
         for side in range(2):
-            project(side, owners[side])
-        return c
-
-    lax.fori_loop(0, T - 2, gather_step, 0)
-    for g in order:
-        ag_copy(g, T - 2, at(-signs[side_of(g)] * (T - 1))).wait_recv()
+            project(owners[side])
+        return c
+
+    lax.fori_loop(0, H - 2, gather_step, 0)
+    owners = [at(-signs[side] * (H - 1)) for side in range(2)]
+    for wanted in (True, False):
+        for side, g in pairs_of:
+            if is_long(side, g) == wanted:
+                ag_copy(side, g, H - 2, owners[side]).wait_recv()
+                if wanted:
+                    ag_copy(side, g, H - 1, owners[side]).start()
     for side in range(2):
-        project(side, at(-signs[side] * (T - 1)))
+        project(owners[side])
+    for side, g in pairs_of:
+        if is_long(side, g):
+            ag_copy(side, g, H - 1, at(H)).wait_recv()
+    project(at(H))
 
     factor = lax.rsqrt(jnp.sum(ssq[...], axis=1, keepdims=True) * (1.0 / D) + EPS)
     pairs = (acc[:, HD:] * factor).astype(BF16)
@@ -266,12 +293,16 @@
         out[half_rows(c), :] = dot_nt(weights, values[:, :seen]).astype(BF16)
 
     def drain(k, c):
-        for g in range(NG):
-            rs_copy(g, k, first.at[rows(g)]).wait_send()
-            ag_copy(g, k, me).wait_send()
-        return c
-
-    lax.fori_loop(0, T - 1, drain, 0)
+        for side, g in pairs_of:
+            rs_copy(side, g, k + 1, first.at[rows(g)]).wait_send()
+            ag_copy(side, g, k, me).wait_send()
+        return c
+
+    lax.fori_loop(0, H - 1, drain, 0)
+    for side, g in pairs_of:
+        if is_long(side, g):
+            rs_copy(side, g, H, first.at[rows(g)]).wait_send()
+            ag_copy(side, g, H - 1, me).wait_send()
     for g in range(NG):
         shift_copy(g).wait_send()
     each_peer(lambda peer: gain_copy(peer, me).wait_send())
@@ -299,18 +330,18 @@
             pltpu.VMEM((KC, D), BF16),
             pltpu.VMEM((D, 2 * HD), BF16),
             pltpu.VMEM((L, B), BF16),
-            pltpu.VMEM((NG, T - 1, L // NG, B), BF16),
+            pltpu.VMEM((2, T // 2, L, B), BF16),
             pltpu.VMEM((L, B), BF16),
             pltpu.VMEM((T, L, B), BF16),
             pltpu.VMEM((T, 1, B), F32),
             pltpu.VMEM((L, 2 * HD), F32),
             pltpu.VMEM((L, HD), F32),
             pltpu.VMEM((T, KC, L), BF16),
-            pltpu.VMEM((L, B), F32),
+            pltpu.VMEM((2, L, B), F32),
             dma((T,)), dma((2,)),
-            dma((NG, T - 1)), dma((NG, T - 1)),
+            dma((2, NG, T // 2)), dma((2, NG, T // 2)),
             dma((NG,)), dma((NG,)),
-            dma((NG, T - 1)), dma((NG, T - 1)),
+            dma((2, NG, T // 2)), dma((2, NG, T // 2)),
             dma((T,)), dma((T,)),
             dma((T,)), dma((T,)),
         ],

time: 99.5 us -> 99.2 us (level)
  no operation moved by 1% of the time
where the time goes in v4:
time: 99.2 us; the launch traced here: 99 us
  Pallas kernels  97.6 us (98%)
  local copies, waits for them, and re-layouts  1.47 us (1%)
    pallas_call x1, Pallas kernels, on_device(): pl.pallas_call(functools.partial(kernel, T, S), out_shape=jax.ShapeDtypeS...  97.6 us

profile of v4, /device:TPU:0, one launch (start us, length us, event | category | flops | bytes accessed | tf_op | source)
XLA Modules:
  0.0 99.0 jit_solution(17113418678364021563)
XLA Ops:
  0.0 97.6 %handover_attention.1 = bf16[256,128]{1,0:T(8,128)(2,1)} custom-call(bf16[256,128]{1,0:T(8,128)(2,1)} %bitcast.13, bf16[256,1024]{1,0:T(8,128)(2,1)} %bitcast.11, f32[1,1024]{1,0:T(1,128)} %gain.1, f32[256,128]{1,0:T(8,128)} %constant.8.clone.cos_q, f32[256,128]{1,0:T(8,128)} %constant.9.clone.sin_q, f32[128,256]{1,0:T(8,128)} %constant.10.clone.cos_k, ...), custom_call_target="tpu_custom_call" | custom-call | flops 1610612736 | bytes 6291456 | tf_op jit(solution)/shard_map/handover_attention/pallas_call | solution.py:323
  97.6 1.5 %copy.12 = bf16[1,256,128]{2,1,0:T(8,128)(2,1)} copy(bf16[1,256,128]{2,1,0:T(8,128)(2,1)} %bitcast.8) | data formatting | bytes 131072

commit v5 on v4

--- a/solution.py
+++ b/solution.py
@@ -36,9 +36,10 @@
 
 def kernel(
     T, S,
-    ctx, res, gain, cos_q, sin_q, cos_k, sin_k, ow_hbm, qw_hbm, kvw_hbm,
+    ctx_hbm, res_hbm, gain_hbm, cos_q_hbm, sin_q_hbm, cos_k_hbm, sin_k_hbm, ow_hbm, qw_hbm, kvw_hbm,
     out,
-    ow, kvw, w, first, rs, hand, xb, gains, acc, ssq, kvall, terms,
+    ctx, res, cos_q, sin_q, cos_k, sin_k,
+    ow, kvw, w, first, rs, hand, base, xb, gains, acc, ssq, kvall, terms,
     ow_sem, load_sem, rs_send, rs_recv, sh_send, sh_recv, ag_send, ag_recv, g_send, g_recv, kv_send, kv_recv,
 ):
     L, HD = ctx.shape
@@ -72,6 +73,8 @@
     def ow_copy(owner):
         return pltpu.make_async_copy(ow_hbm.at[:, block(owner)], ow.at[:, block(owner)], ow_sem.at[owner])
 
+    ctx_load = pltpu.make_async_copy(ctx_hbm, ctx, load_sem.at[2])
+    ctx_load.start()
     ow_copy(at(H)).start()
     ow_copy(at(H - 1)).start()
     ow_copy(at(1 - H)).start()
@@ -90,6 +93,19 @@
     q_load = pltpu.make_async_copy(qw_hbm, w.at[:, pl.ds(0, HD)], load_sem.at[1])
     q_load.start()
 
+    gain_load = pltpu.make_async_copy(gain_hbm, gains.at[me], load_sem.at[3])
+    gain_load.start()
+    res_load = pltpu.make_async_copy(res_hbm, res, load_sem.at[4])
+    res_load.start()
+    table_loads = [
+        pltpu.make_async_copy(source, target, load_sem.at[5 + i])
+        for i, (source, target) in enumerate(
+            ((cos_q_hbm, cos_q), (sin_q_hbm, sin_q), (cos_k_hbm, cos_k), (sin_k_hbm, sin_k))
+        )
+    ]
+    for load in table_loads:
+        load.start()
+
     barrier = pltpu.get_barrier_semaphore()
 
     def each_peer(act):
@@ -103,8 +119,10 @@
         pl.semaphore_signal(barrier, inc=1, device_id=(s, t), device_id_type=MESH)
 
     each_peer(lambda peer: greet(sec, peer))
-    greet(following, me)
-    greet(previous, me)
+    for section in (following, previous):
+        greet(section, me)
+        for side in range(2):
+            greet(section, sides[side])
 
     def rows(g):
         return pl.ds(g * R, R)
@@ -115,16 +133,16 @@
     order = [g for j in range(NG // 2) for g in (j, j + NG // 2)]
     pairs_of = [(side, g) for g in order for side in range(2)]
 
-    def rs_copy(side, g, left, source):
+    def rs_copy(side, g, left, source, section=None):
         return pltpu.make_async_remote_copy(
             src_ref=source, dst_ref=rs.at[side, left - 1, rows(g)],
             send_sem=rs_send.at[side, g, left - 1], recv_sem=rs_recv.at[side, g, left - 1],
-            device_id=(sec, sides[side]), device_id_type=MESH,
+            device_id=(sec if section is None else section, sides[side]), device_id_type=MESH,
         )
 
     def shift_copy(g):
         return pltpu.make_async_remote_copy(
-            src_ref=hand.at[rows(g)], dst_ref=xb.at[me, rows(g)], send_sem=sh_send.at[g], recv_sem=sh_recv.at[g],
+            src_ref=hand.at[rows(g)], dst_ref=base.at[rows(g)], send_sem=sh_send.at[g], recv_sem=sh_recv.at[g],
             device_id=(following, me), device_id_type=MESH,
         )
 
@@ -137,7 +155,7 @@
 
     def gain_copy(peer, slot):
         return pltpu.make_async_remote_copy(
-            src_ref=gain, dst_ref=gains.at[slot], send_sem=g_send.at[peer], recv_sem=g_recv.at[slot],
+            src_ref=gains.at[me], dst_ref=gains.at[slot], send_sem=g_send.at[peer], recv_sem=g_recv.at[slot],
             device_id=(sec, peer), device_id_type=MESH,
         )
 
@@ -168,9 +186,10 @@
             [jnp.transpose(kvw[:, block(i)]), jnp.zeros((B, HD - KC), BF16)], axis=1
         )
 
+    ctx_load.wait()
     ow_copy(at(H)).wait()
     first[...] = term(at(H)).astype(BF16)
-    pl.semaphore_wait(barrier, T + 1)
+    pl.semaphore_wait(barrier, T + 5)
     for side, g in pairs_of:
         if is_long(side, g):
             rs_copy(side, g, H, first.at[rows(g)]).start()
@@ -182,7 +201,7 @@
         if not is_long(side, g):
             rs[side, H - 1, rows(g), :] = terms[side, rows(g), :].astype(BF16)
             rs_copy(side, g, H - 1, rs.at[side, H - 1, rows(g)]).start()
-    gains[me] = gain[...]
+    gain_load.wait()
     each_peer(lambda peer: gain_copy(peer, me).start())
 
     for side, g in pairs_of:
@@ -195,40 +214,47 @@
     lax.fori_loop(T + 2 - H, T + H - 1, wait_rest, 0)
     for side in range(2):
         terms[side] = term(at(signs[side] * (H - 2)))
+    res_load.wait()
+    hand[...] = (term(me) + res[...].astype(F32)).astype(BF16)
+    for g in order:
+        shift_copy(g).start()
     acc[...] = jnp.zeros_like(acc)
     ssq[...] = jnp.zeros_like(ssq)
     kv_load.wait()
     place(T - 2)
     place(T - 1)
 
-    def reduce_step(i, c):
-        left = H - 2 - i
+    def pass_sums(left, section=None):
         for side, g in pairs_of:
             rs_copy(side, g, left + 1, first.at[rows(g)]).wait_recv()
             total = rs[side, left, rows(g), :].astype(F32) + terms[side, rows(g), :]
             rs[side, left, rows(g), :] = total.astype(BF16)
-            rs_copy(side, g, left, rs.at[side, left, rows(g)]).start()
+            rs_copy(side, g, left, rs.at[side, left, rows(g)], section).start()
+
+    def reduce_step(i, c):
+        left = H - 2 - i
+        pass_sums(left)
         for side in range(2):
             terms[side] = term(at(signs[side] * (left - 1)))
         for n in range(2):
             place(2 * i + n)
         return c
 
-    lax.fori_loop(0, H - 2, reduce_step, 0)
-    terms[0] += res[...].astype(F32)
-    for g in order:
-        for side in range(2):
-            rs_copy(side, g, 1, first.at[rows(g)]).wait_recv()
-        total = rs[0, 0, rows(g), :].astype(F32) + rs[1, 0, rows(g), :].astype(F32) + terms[0, rows(g), :]
-        hand[rows(g), :] = total.astype(BF16)
-        shift_copy(g).start()
-    place(T - 4)
-    place(T - 3)
+    lax.fori_loop(0, H - 3, reduce_step, 0)
+    pass_sums(1, following)
+    for i in range(T - 6, T - 2):
+        place(i)
 
     each_peer(lambda peer: gain_copy(peer, peer).wait_recv())
     q_load.wait()
+    for load in table_loads:
+        load.wait()
     for g in order:
         shift_copy(g).wait_recv()
+        for side in range(2):
+            rs_copy(side, g, 1, first.at[rows(g)], following).wait_recv()
+        total = base[rows(g), :].astype(F32) + rs[0, 0, rows(g), :].astype(F32) + rs[1, 0, rows(g), :].astype(F32)
+        xb[me, rows(g), :] = total.astype(BF16)
         for side in range(2):
             ag_copy(side, g, 0, me).start()
     project(me)
@@ -318,19 +344,26 @@
     KC = kv_weight.shape[2]
     tables = rope_tables(L, HD)
     vmem = pl.BlockSpec(memory_space=pltpu.VMEM)
-    anywhere = pl.BlockSpec(memory_space=pl.ANY)
+    hbm = pl.BlockSpec(memory_space=pltpu.HBM)
     dma = pltpu.SemaphoreType.DMA
     attended = pl.pallas_call(
         functools.partial(kernel, T, S),
         out_shape=jax.ShapeDtypeStruct((L, HD), BF16),
-        in_specs=[vmem] * 7 + [anywhere] * 3,
+        in_specs=[hbm] * 10,
         out_specs=vmem,
         scratch_shapes=[
+            pltpu.VMEM((L, HD), BF16),
+            pltpu.VMEM((L, B), BF16),
+            pltpu.VMEM((L, HD), F32),
+            pltpu.VMEM((L, HD), F32),
+            pltpu.VMEM((HD, L), F32),
+            pltpu.VMEM((HD, L), F32),
             pltpu.VMEM((HD, D), BF16),
             pltpu.VMEM((KC, D), BF16),
             pltpu.VMEM((D, 2 * HD), BF16),
             pltpu.VMEM((L, B), BF16),
             pltpu.VMEM((2, T // 2, L, B), BF16),
+            pltpu.VMEM((L, B), BF16),
             pltpu.VMEM((L, B), BF16),
             pltpu.VMEM((T, L, B), BF16),
             pltpu.VMEM((T, 1, B), F32),
@@ -338,7 +371,7 @@
             pltpu.VMEM((L, HD), F32),
             pltpu.VMEM((T, KC, L), BF16),
             pltpu.VMEM((2, L, B), F32),
-            dma((T,)), dma((2,)),
+            dma((T,)), dma((9,)),
             dma((2, NG, T // 2)), dma((2, NG, T // 2)),
             dma((NG,)), dma((NG,)),
             dma((2, NG, T // 2)), dma((2, NG, T // 2)),

time: 99.2 us -> 96.8 us (0.976)
  Pallas kernels: 97.6 us -> 95.2 us
    pallas_call x1, Pallas kernels: 97.6 us -> 95.2 us  [on_device(): pl.pallas_call(functools.partial(kernel, T, S), out_shape=jax.ShapeDtypeS...]
where the time goes in v5:
time: 96.8 us; the launch traced here: 96.6 us
  Pallas kernels  95.2 us (98%)
  local copies, waits for them, and re-layouts  1.47 us (2%)
    pallas_call x1, Pallas kernels, on_device(): pl.pallas_call(functools.partial(kernel, T, S), out_shape=jax.ShapeDtypeS...  95.2 us

profile of v5, /device:TPU:0, one launch (start us, length us, event | category | flops | bytes accessed | tf_op | source)
XLA Modules:
  0.0 96.6 jit_solution(2166295136828034361)
XLA Ops:
  0.0 95.2 %handover_attention.1 = bf16[256,128]{1,0:T(8,128)(2,1)} custom-call(bf16[256,128]{1,0:T(8,128)(2,1)} %bitcast.13, bf16[256,1024]{1,0:T(8,128)(2,1)} %bitcast.11, f32[1,1024]{1,0:T(1,128)} %gain_hbm.1, f32[256,128]{1,0:T(8,128)} %constant.8.clone.cos_q_hbm, f32[256,128]{1,0:T(8,128)} %constant.9.clone.sin_q_hbm, f32[128,256]{1,0:T(8,128)} %constant.10.clone.cos_k_hbm, ...), custom_call_target="tpu_custom_call" | custom-call | flops 1610612736 | bytes 6291456 | tf_op jit(solution)/shard_map/handover_attention/pallas_call | solution.py:349
  95.2 1.5 %copy.12 = bf16[1,256,128]{2,1,0:T(8,128)(2,1)} copy(bf16[1,256,128]{2,1,0:T(8,128)(2,1)} %bitcast.8) | data formatting | bytes 131072

commit v6 on v5

--- a/solution.py
+++ b/solution.py
@@ -132,6 +132,8 @@
 
     order = [g for j in range(NG // 2) for g in (j, j + NG // 2)]
     pairs_of = [(side, g) for g in order for side in range(2)]
+    longs = [pair for pair in pairs_of if is_long(*pair)]
+    shorts = [pair for pair in pairs_of if not is_long(*pair)]
 
     def rs_copy(side, g, left, source, section=None):
         return pltpu.make_async_remote_copy(
@@ -225,7 +227,7 @@
     place(T - 1)
 
     def pass_sums(left, section=None):
-        for side, g in pairs_of:
+        for side, g in shorts + longs:
             rs_copy(side, g, left + 1, first.at[rows(g)]).wait_recv()
             total = rs[side, left, rows(g), :].astype(F32) + terms[side, rows(g), :]
             rs[side, left, rows(g), :] = total.astype(BF16)
@@ -256,12 +258,15 @@
         total = base[rows(g), :].astype(F32) + rs[0, 0, rows(g), :].astype(F32) + rs[1, 0, rows(g), :].astype(F32)
         xb[me, rows(g), :] = total.astype(BF16)
         for side in range(2):
-            ag_copy(side, g, 0, me).start()
+            if is_long(side, g):
+                ag_copy(side, g, 0, me).start()
+    for side, g in shorts:
+        ag_copy(side, g, 0, me).start()
     project(me)
 
     def gather_step(k, c):
         owners = [at(-signs[side] * (1 + k)) for side in range(2)]
-        for side, g in pairs_of:
+        for side, g in longs + shorts:
             ag_copy(side, g, k, owners[side]).wait_recv()
             ag_copy(side, g, k + 1, owners[side]).start()
         for side in range(2):

time: 96.8 us -> 96.8 us (level)
  no operation moved by 1% of the time
where the time goes in v6:
time: 96.8 us; the launch traced here: 96.6 us
  Pallas kernels  95.2 us (98%)
  local copies, waits for them, and re-layouts  1.47 us (2%)
    pallas_call x1, Pallas kernels, on_device(): pl.pallas_call(functools.partial(kernel, T, S), out_shape=jax.ShapeDtypeS...  95.2 us

profile of v6, /device:TPU:0, one launch (start us, length us, event | category | flops | bytes accessed | tf_op | source)
XLA Modules:
  0.0 96.6 jit_solution(14672676095175635102)
XLA Ops:
  0.0 95.2 %handover_attention.1 = bf16[256,128]{1,0:T(8,128)(2,1)} custom-call(bf16[256,128]{1,0:T(8,128)(2,1)} %bitcast.13, bf16[256,1024]{1,0:T(8,128)(2,1)} %bitcast.11, f32[1,1024]{1,0:T(1,128)} %gain_hbm.1, f32[256,128]{1,0:T(8,128)} %constant.8.clone.cos_q_hbm, f32[256,128]{1,0:T(8,128)} %constant.9.clone.sin_q_hbm, f32[128,256]{1,0:T(8,128)} %constant.10.clone.cos_k_hbm, ...), custom_call_target="tpu_custom_call" | custom-call | flops 1610612736 | bytes 6291456 | tf_op jit(solution)/shard_map/handover_attention/pallas_call | solution.py:354
  95.2 1.5 %copy.12 = bf16[1,256,128]{2,1,0:T(8,128)(2,1)} copy(bf16[1,256,128]{2,1,0:T(8,128)(2,1)} %bitcast.8) | data formatting | bytes 131072

commit v7 on v6

--- a/solution.py
+++ b/solution.py
@@ -14,7 +14,7 @@
 MESH = pl.DeviceIdType.MESH
 BF16 = jnp.bfloat16
 F32 = jnp.float32
-NG = 4
+NG = 8
 
 
 def rope_tables(length, head_size):

time: 96.8 us -> 98.2 us (1.014)
  Pallas kernels: 95.2 us -> 96.5 us
    pallas_call x1, Pallas kernels: 95.2 us -> 96.5 us  [on_device(): pl.pallas_call(functools.partial(kernel, T, S), out_shape=jax.ShapeDtypeS...]
where the time goes in v7:
time: 98.2 us; the launch traced here: 98 us
  Pallas kernels  96.5 us (98%)
  local copies, waits for them, and re-layouts  1.47 us (1%)
    pallas_call x1, Pallas kernels, on_device(): pl.pallas_call(functools.partial(kernel, T, S), out_shape=jax.ShapeDtypeS...  96.5 us

profile of v7, /device:TPU:0, one launch (start us, length us, event | category | flops | bytes accessed | tf_op | source)
XLA Modules:
  0.0 98.0 jit_solution(13179235153236654721)
XLA Ops:
  0.0 96.5 %handover_attention.1 = bf16[256,128]{1,0:T(8,128)(2,1)} custom-call(bf16[256,128]{1,0:T(8,128)(2,1)} %bitcast.13, bf16[256,1024]{1,0:T(8,128)(2,1)} %bitcast.11, f32[1,1024]{1,0:T(1,128)} %gain_hbm.1, f32[256,128]{1,0:T(8,128)} %constant.8.clone.cos_q_hbm, f32[256,128]{1,0:T(8,128)} %constant.9.clone.sin_q_hbm, f32[128,256]{1,0:T(8,128)} %constant.10.clone.cos_k_hbm, ...), custom_call_target="tpu_custom_call" | custom-call | flops 1610612736 | bytes 6291456 | tf_op jit(solution)/shard_map/handover_attention/pallas_call | solution.py:354
  96.5 1.5 %copy.12 = bf16[1,256,128]{2,1,0:T(8,128)(2,1)} copy(bf16[1,256,128]{2,1,0:T(8,128)(2,1)} %bitcast.8) | data formatting | bytes 131072
